TPU v7x, 256 devices: a whole 4x4x8 slice. The times are simulated.
256 devices in a mesh: dom: 8 (over z), row: 16 (over y, x), col: 2 (over core).
Axes of the slice: x: 4, y: 4, z: 8, core: 2. Of those that a mesh axis runs over, the one named last changes fastest.
Arguments:
- next_inverse: bfloat16 [8, 4096, 4096], P('dom', 'row', 'col'), may hold values from -6 to 6
- next_arrow: bfloat16 [8, 64, 4096], P('dom', None, 'row'), may hold values from -6 to 6
- factor_win: bfloat16 [8, 4096, 3072], P('dom', 'row', 'col'), may hold values from -0.09375 to 0.09375
- factor_rest: bfloat16 [8, 4096, 1024], P('dom', 'row', 'col'), may hold values from -0.09375 to 0.09375
- arrow_win: bfloat16 [8, 64, 3072], P('dom', None, 'col'), may hold values from -0.75 to 0.75
- arrow_rest: bfloat16 [8, 64, 1024], P('dom', None, 'col'), may hold values from -0.75 to 0.75
- tip_inverse: bfloat16 [64, 64], replicated, may hold values from -6 to 6
- base_win: bfloat16 [8, 3072, 3072], P('dom', 'row', 'col'), may hold values from -6 to 6
- base_rest: bfloat16 [8, 3072, 1024], P('dom', 'row', 'col'), may hold values from -6 to 6
Outputs:
- sub_inverse: bfloat16 [8, 4096, 3072], P('dom', 'row', 'col')
- arrow_inverse: bfloat16 [8, 64, 3072], P('dom', None, 'col')
- diag_win: bfloat16 [8, 3072, 3072], P('dom', 'row', 'col')
- diag_rest: bfloat16 [8, 3072, 1024], P('dom', 'row', 'col')
All inputs are finite; a program needn't handle non-finite values.
Results may differ from a plain program's by a relative error of at most 0.0046.
Values may be sent and summed in bfloat16 or wider, within the bound.
A program may use at most 128 MiB of HBM per device.

v0:
```python
import jax
import jax.numpy as jnp
from jax import lax
from jax.sharding import PartitionSpec as P


def shifted(value, axis, steps):
    count = lax.axis_size(axis)
    leading, last = (max(0, -steps), min(count, count - steps))
    return lax.ppermute(value, axis, [(source, source + steps) for source in range(leading, last)])


def contract_first(left, right):
    return lax.dot_general(
        left, right, (((0,), (0,)), ((), ())), preferred_element_type=jnp.float32
    )


def per_device(
    next_inverse,
    next_arrow,
    factor_win,
    factor_rest,
    arrow_win,
    arrow_rest,
    tip_inverse,
    base_win,
    base_rest,
):
    inverse_tile = next_inverse[0]
    arrow_tile = next_arrow[0]
    factor_tile = factor_win[0]
    factor_other = factor_rest[0]
    ratio_tile = arrow_win[0]
    ratio_other = arrow_rest[0]
    factor_column = lax.all_gather(factor_tile, "row", axis=0, tiled=True)
    inverse_next, arrow_next = shifted((inverse_tile, arrow_tile), "dom", -1)
    start_sum = contract_first(arrow_next, ratio_tile)
    x_total = start_sum + jnp.dot(
        lax.all_gather(inverse_next, "col", axis=1, tiled=True),
        factor_column,
        preferred_element_type=jnp.float32,
    )
    x_bf = x_total.astype(jnp.bfloat16)
    y_part = jnp.dot(arrow_next, factor_tile, preferred_element_type=jnp.float32)
    y_total = lax.psum(y_part, "row") + jnp.dot(
        tip_inverse, ratio_tile, preferred_element_type=jnp.float32
    )
    y_bf = y_total.astype(jnp.bfloat16)
    x_panel, y_panel = (
        lax.all_gather(x_bf, "col", axis=1, tiled=True),
        lax.all_gather(y_bf, "col", axis=1, tiled=True),
    )
    ratio_both = jnp.concatenate([ratio_tile, ratio_other], axis=1)
    rows_here = y_panel.shape[1] // lax.axis_size("row")
    y_rows = lax.dynamic_slice_in_dim(y_panel, lax.axis_index("row") * rows_here, rows_here, 1)
    x_columns = lax.all_to_all(x_panel, "row", split_axis=1, concat_axis=0, tiled=True)
    rest_column = lax.all_gather(factor_other, "row", axis=0, tiled=True)
    factor_full = jnp.concatenate([factor_column, rest_column], axis=1)
    diag_part = contract_first(x_columns, factor_full)
    base_both = jnp.concatenate([base_win[0], base_rest[0]], axis=1).astype(jnp.float32)
    diag_total = base_both + diag_part + contract_first(y_rows, ratio_both)
    split = factor_tile.shape[1]
    diag_left = diag_total[:, :split].astype(jnp.bfloat16)
    diag_right = diag_total[:, split:].astype(jnp.bfloat16)
    return ((-x_bf)[None], (-y_bf)[None], diag_left[None], diag_right[None])


def solution(mesh):
    in_specs = (
        P("dom", "row", "col"),
        P("dom", None, "row"),
        P("dom", "row", "col"),
        P("dom", "row", "col"),
        P("dom", None, "col"),
        P("dom", None, "col"),
        P(),
        P("dom", "row", "col"),
        P("dom", "row", "col"),
    )
    out_specs = (
        P("dom", "row", "col"),
        P("dom", None, "col"),
        P("dom", "row", "col"),
        P("dom", "row", "col"),
    )
    return jax.shard_map(
        per_device, mesh=mesh, in_specs=in_specs, out_specs=out_specs, check_vma=False
    )
```

profile of v0, /device:TPU:1, one launch (start us, length us, event | category | flops | bytes accessed | tf_op | source)
XLA Modules:
  0.0 360.3 jit_solution(10407591954021950761)
XLA Ops:
  7.2 0.0 copy-start
  7.2 0.0 copy-start.7
  7.2 0.0 all-gather.7.cloned.1.call-start
  7.2 1.3 collective-permute-start.1
  8.5 24.2 %collective-permute-done.1 = bf16[256,2048]{1,0:T(8,128)(2,1)S(1)} collective-permute-done((bf16[256,2048]{1,0:T(8,128)(2,1)}, bf16[256,2048]{1,0:T(8,128)(2,1)S(1)}, u32[]{:S(2)}, u32[]{:S(2)}) %collective-permute-start.1) | collective-permute-done | bytes 1048608 | tf_op jit(solution)/shard_map/ppermute | solution.py:10
  32.8 0.0 copy-start.4
  32.8 1.0 copy-done.4
  33.8 0.0 all-gather.7.cloned.1.call-update
  33.8 0.0 all-gather.11.cloned.1.call-start
  33.9 0.7 all-gather.11.cloned.1.call-update
  34.6 0.0 all-gather.9.cloned.1.call-start
  34.6 0.0 copy-done.7
  34.6 0.0 copy-start.3
  34.6 1.4 collective-permute-start
  36.1 19.8 %all-gather.7.cloned.1.call-done = bf16[256,4096]{1,0:T(8,128)(2,1)} async-done(((bf16[256,2048]{1,0:T(8,128)(2,1)}), bf16[256,4096]{1,0:T(8,128)(2,1)}) %all-gather.7.cloned.1.call-update) | async-done | bytes 2097168 | tf_op jit(solution)/shard_map/all_gather | solution.py:40
  55.9 98.0 %all-gather.11.cloned.1.call-done = bf16[1,4096,1536]{2,1,0:T(8,128)(2,1)} async-done(((bf16[1,256,1536]{2,1,0:T(8,128)(2,1)}), bf16[1,4096,1536]{2,1,0:T(8,128)(2,1)}) %all-gather.11.cloned.1.call-update) | async-done | bytes 12582928 | tf_op jit(solution)/shard_map/all_gather | solution.py:36
  153.9 7.0 %fusion.18 = f32[256,1536]{1,0:T(8,128)S(1)} fusion(bf16[256,4096]{1,0:T(8,128)(2,1)} %all-gather.7.cloned.1.call-done, bf16[1,4096,1536]{2,1,0:T(8,128)(2,1)} %all-gather.11.cloned.1.call-done), kind=kOutput, calls=%fused_computation.23 | convolution fusion | flops 3221225472 | bytes 16252928 | tf_op jit(solution)/shard_map/dot_general | solution.py:39
  160.9 0.0 copy-start.2
  160.9 0.0 collective-permute-done
  161.0 0.0 copy-done.3
  161.0 1.3 fusion.4
  162.2 0.0 all-gather.9.cloned.1.call-update
  162.3 0.0 all-reduce.2.cloned.1.call-start
  162.3 0.0 copy-done.2
  162.3 1.0 fusion.9
  163.3 0.0 all-reduce.2.cloned.1.call-update
  163.3 0.0 all-gather.13.cloned.1.call-start
  163.4 0.5 all-gather.13.cloned.1.call-update
  163.9 14.1 %all-gather.9.cloned.1.call-done = bf16[256,3072]{1,0:T(8,128)(2,1)} async-done(((bf16[256,1536]{1,0:T(8,128)(2,1)}), bf16[256,3072]{1,0:T(8,128)(2,1)}) %all-gather.9.cloned.1.call-update) | async-done | bytes 1572880 | tf_op jit(solution)/shard_map/all_gather | solution.py:51
  178.0 2.6 copy.13
  180.6 6.3 %all-to-all-start = ((bf16[256,16,192]{0,2,1:T(8,128)(2,1)}), bf16[256,16,192]{0,2,1:T(8,128)(2,1)S(1)}, u32[]{:S(2)}, u32[]{:S(2)}) async-start(bf16[256,16,192]{0,2,1:T(8,128)(2,1)} %bitcast.9), calls=%async_computation | async-start | bytes 3145728 | tf_op jit(solution)/shard_map/all_to_all | solution.py:57
  186.9 0.0 copy-start.1
  186.9 0.0 copy-done
  186.9 0.2 fusion.20
  187.1 95.9 %all-reduce.2.cloned.1.call-done = f32[64,1536]{1,0:T(8,128)} async-done(((f32[64,1536]{1,0:T(8,128)}), f32[64,1536]{1,0:T(8,128)}) %all-reduce.2.cloned.1.call-update) | async-done | bytes 393232 | tf_op jit(solution)/shard_map/psum | solution.py:46
  283.0 1.7 negate_bitcast_fusion.1
  284.7 3.8 %all_gather.19 = bf16[64,3072]{1,0:T(8,128)(2,1)} all-gather(bf16[64,1536]{1,0:T(8,128)(2,1)S(1)} %get-tuple-element.5), channel_id=1, replica_groups=mesh['dom'=8,'row'=16,'col'=2] {'col'}, dimensions={1}, use_global_device_ids=true | all-gather | bytes 589824 | tf_op jit(solution)/shard_map/all_gather | solution.py:52
  288.5 0.0 copy-done.1
  288.5 0.9 negate_bitcast_fusion
  289.4 0.0 all-to-all-done
  289.4 0.2 copy.15
  289.6 53.0 %all-gather.13.cloned.1.call-done = bf16[1,4096,512]{2,1,0:T(8,128)(2,1)} async-done(((bf16[1,256,512]{2,1,0:T(8,128)(2,1)}), bf16[1,4096,512]{2,1,0:T(8,128)(2,1)}) %all-gather.13.cloned.1.call-update) | async-done | bytes 4194320 | tf_op jit(solution)/shard_map/all_gather | solution.py:58
  342.6 0.0 copy-done.6
  342.6 8.4 %fusion.5 = f32[192,2048]{1,0:T(8,128)S(1)} fusion(bf16[4096,192]{0,1:T(8,128)(2,1)S(1)} %bitcast.36, bf16[4096,512]{1,0:T(8,128)(2,1)} %bitcast.39, bf16[4096,1536]{1,0:T(8,128)(2,1)} %bitcast.38, bf16[192,512]{1,0:T(8,128)(2,1)S(1)} %bitcast.42, bf16[192,1536]{1,0:T(8,128)(2,1)} %bitcast.41), kind=kOutput, calls=%fused_computation.7 | convolution fusion | flops 3256745984 | bytes 20709376 | tf_op jit(solution)/shard_map/dot_general | solution.py:14
  350.9 0.0 copy-done.5
  351.0 1.3 fusion.8
  352.2 0.9 slice_bitcast_fusion
  353.1 0.7 slice_bitcast_fusion.1
  (2 shorter events, 0.0 us)
Async XLA Ops:
  7.2 179.7 %copy-start = (bf16[64,64]{1,0:T(8,128)(2,1)S(1)}, bf16[64,64]{1,0:T(8,128)(2,1)}, u32[]{:S(2)}) copy-start(bf16[64,64]{1,0:T(8,128)(2,1)} %param.15) | copy-start | bytes 24580
  7.2 27.4 %copy-start.7 = (bf16[1,64,256]{2,1,0:T(8,128)(2,1)S(1)}, bf16[1,64,256]{2,1,0:T(8,128)(2,1)}, u32[]{:S(2)}) copy-start(bf16[1,64,256]{2,1,0:T(8,128)(2,1)} %param.10) | copy-start | bytes 98308
  7.2 48.7 %all-gather.7.cloned.1.call-start = ((), (), s32[]{:S(2)}) async-start(), calls=%async_computation.1 | async-start | bytes 3145728 | tf_op jit(solution)/shard_map/all_gather | solution.py:40
  7.2 25.5 %collective-permute-start.1 = (bf16[256,2048]{1,0:T(8,128)(2,1)}, bf16[256,2048]{1,0:T(8,128)(2,1)S(1)}, u32[]{:S(2)}, u32[]{:S(2)}) collective-permute-start(bf16[256,2048]{1,0:T(8,128)(2,1)} %bitcast.40), channel_id=1, source_target_pairs={{32,0},{64,32},{96,64},{128,96},{160,128},{192,160},{224,192},{33,... | collective-permute-start | bytes 3145736 | tf_op jit(solution)/shard_map/ppermute | solution.py:10
  32.8 1.0 copy-start.4
  33.8 120.1 %all-gather.11.cloned.1.call-start = ((), (), s32[]{:S(2)}) async-start(), calls=%async_computation.4 | async-start | bytes 13369344 | tf_op jit(solution)/shard_map/all_gather | solution.py:36
  34.6 143.5 %all-gather.9.cloned.1.call-start = ((), (), s32[]{:S(2)}) async-start(), calls=%async_computation.3 | async-start | bytes 2359296 | tf_op jit(solution)/shard_map/all_gather | solution.py:51
  34.6 126.3 %copy-start.3 = (bf16[1,64,1536]{2,1,0:T(8,128)(2,1)S(1)}, bf16[1,64,1536]{2,1,0:T(8,128)(2,1)}, u32[]{:S(2)}) copy-start(bf16[1,64,1536]{2,1,0:T(8,128)(2,1)} %param.13) | copy-start | bytes 589828
  34.6 126.3 %collective-permute-start = (bf16[64,256]{1,0:T(8,128)(2,1)S(1)}, bf16[64,256]{1,0:T(8,128)(2,1)S(1)}, u32[]{:S(2)}, u32[]{:S(2)}) collective-permute-start(bf16[64,256]{1,0:T(8,128)(2,1)S(1)} %bitcast.43), channel_id=1, source_target_pairs={{32,0},{64,32},{96,64},{128,96},{160,128},{192,160},{224,192},{33,... | collective-permute-start | bytes 98312 | tf_op jit(solution)/shard_map/ppermute | solution.py:10
  160.9 1.4 copy-start.2
  162.3 120.7 %all-reduce.2.cloned.1.call-start = ((), (), s32[]{:S(2)}) async-start(), calls=%async_computation.2 | async-start | bytes 786432 | tf_op jit(solution)/shard_map/psum | solution.py:46
  163.3 179.2 %all-gather.13.cloned.1.call-start = ((), (), s32[]{:S(2)}) async-start(), calls=%async_computation.5 | async-start | bytes 4456448 | tf_op jit(solution)/shard_map/all_gather | solution.py:58
  180.6 108.8 %all-to-all-start = ((bf16[256,16,192]{0,2,1:T(8,128)(2,1)}), bf16[256,16,192]{0,2,1:T(8,128)(2,1)S(1)}, u32[]{:S(2)}, u32[]{:S(2)}) async-start(bf16[256,16,192]{0,2,1:T(8,128)(2,1)} %bitcast.9), calls=%async_computation | async-start | bytes 3145728 | tf_op jit(solution)/shard_map/all_to_all | solution.py:57
  186.9 101.6 %copy-start.1 = (bf16[256,1536]{1,0:T(8,128)(2,1)S(1)}, bf16[256,1536]{1,0:T(8,128)(2,1)}, u32[]{:S(2)}) copy-start(bf16[256,1536]{1,0:T(8,128)(2,1)} %fusion.4) | copy-start | bytes 2359300
  289.4 53.1 %copy-start.6 = (bf16[1,192,512]{2,1,0:T(8,128)(2,1)S(1)}, bf16[1,192,512]{2,1,0:T(8,128)(2,1)}, u32[]{:S(2)}) copy-start(bf16[1,192,512]{2,1,0:T(8,128)(2,1)} %param.17) | copy-start | bytes 589828
  342.6 8.4 %copy-start.5 = (bf16[1,64,512]{2,1,0:T(8,128)(2,1)S(1)}, bf16[1,64,512]{2,1,0:T(8,128)(2,1)}, u32[]{:S(2)}) copy-start(bf16[1,64,512]{2,1,0:T(8,128)(2,1)} %param.14) | copy-start | bytes 196612
Sparse Core Ops, SparseCore 0:
  33.9 21.8 all-gather.6
  58.3 95.5 all-gather.10
  162.4 15.6 all-gather.8
  181.7 101.2 all-reduce.1
  285.3 57.2 all-gather.12
where the time goes:
time: 361 us; the launch traced here: 360 us
  waiting for transfers between devices  306 us (85%)
  matrix products  19.1 us (5%)
  between operations  13.9 us (4%)
  starting transfers between devices  9.18 us (3%)
  local copies, waits for them, and re-layouts  5.35 us (1%)
  blocking collectives  3.8 us (1%)
    all_gather x1, waiting for transfers between devices, per_device(): factor_column = lax.all_gather(factor_tile, 'row', axis=0, tiled=True)  98 us
    psum x1, waiting for transfers between devices, per_device(): lax.psum(y_part, 'row')  95.9 us
    all_gather x1, waiting for transfers between devices, per_device(): rest_column = lax.all_gather(factor_other, 'row', axis=0, tiled=True)  53 us
    ppermute x2, waiting for transfers between devices, shifted(): lax.ppermute(value, axis, [(source, source + steps) for source in range(l...  24.2 us
    all_gather x1, waiting for transfers between devices, per_device(): lax.all_gather(inverse_next, 'col', axis=1, tiled=True)  19.8 us
    all_gather x1, waiting for transfers between devices, per_device(): lax.all_gather(x_bf, 'col', axis=1, tiled=True)  14.1 us
    dot_general x3, matrix products, contract_first(): lax.dot_general(left, right, (((0,), (0,)), ((), ())), preferred_element_...  10.9 us
  transfers between devices with their start and end apart: 8, of which 6 were waited for; matrix products, arithmetic and copies ran while one was open for 4% of the time, Pallas kernels for 0%

commit v1 on v0

--- a/solution.py
+++ b/solution.py
@@ -2,6 +2,15 @@
 import jax.numpy as jnp
 from jax import lax
 from jax.sharding import PartitionSpec as P
+from jax.lax import all_to_all, psum
+
+
+def _balance_modes(original, array_axis=1):
+    r2 = jnp.concatenate(
+        all_to_all(jnp.stack([original for _ in range(psum(1, "col"))], axis=0), "col", 0, 0),
+        axis=array_axis,
+    )
+    return r2
 
 
 def shifted(value, axis, steps):
@@ -37,9 +46,7 @@
     inverse_next, arrow_next = shifted((inverse_tile, arrow_tile), "dom", -1)
     start_sum = contract_first(arrow_next, ratio_tile)
     x_total = start_sum + jnp.dot(
-        lax.all_gather(inverse_next, "col", axis=1, tiled=True),
-        factor_column,
-        preferred_element_type=jnp.float32,
+        _balance_modes(inverse_next), factor_column, preferred_element_type=jnp.float32
     )
     x_bf = x_total.astype(jnp.bfloat16)
     y_part = jnp.dot(arrow_next, factor_tile, preferred_element_type=jnp.float32)

time: 361 us -> 316 us (0.88)
  waiting for transfers between devices: 306 us -> 253 us
  blocking collectives: 3.8 us -> 12.2 us
    all_gather x1, waiting for transfers between devices: 98 us -> 65.8 us  [per_device(): factor_column = lax.all_gather(factor_tile, 'row', axis=0, tiled=True)]
    all_gather x1 -> x0, waiting for transfers between devices: 19.8 us -> none  [per_device(): lax.all_gather(inverse_next, 'col', axis=1, tiled=True)]
    all_to_all x0 -> x1, blocking collectives: none -> 8.44 us  [_balance_modes(): all_to_all(jnp.stack([original for _ in range(psum(1, 'col'))], axis=0),...]
  transfers between devices with their start and end apart: 8 -> 7, of which waited for: 6 -> 5; matrix products, arithmetic and copies ran while one was open for 4% -> 5% of each run, Pallas kernels for 0% -> 0%
where the time goes in v1:
time: 316 us; the launch traced here: 315 us
  waiting for transfers between devices  253 us (80%)
  matrix products  18.6 us (6%)
  between operations  13.9 us (4%)
  blocking collectives  12.2 us (4%)
  starting transfers between devices  9.14 us (3%)
  local copies, waits for them, and re-layouts  5.82 us (2%)
    psum x1, waiting for transfers between devices, per_device(): lax.psum(y_part, 'row')  95.9 us
    all_gather x1, waiting for transfers between devices, per_device(): factor_column = lax.all_gather(factor_tile, 'row', axis=0, tiled=True)  65.8 us
    all_gather x1, waiting for transfers between devices, per_device(): rest_column = lax.all_gather(factor_other, 'row', axis=0, tiled=True)  53 us
    ppermute x2, waiting for transfers between devices, shifted(): lax.ppermute(value, axis, [(source, source + steps) for source in range(l...  22.8 us
    all_gather x1, waiting for transfers between devices, per_device(): lax.all_gather(x_bf, 'col', axis=1, tiled=True)  14.1 us
    dot_general x3, matrix products, contract_first(): lax.dot_general(left, right, (((0,), (0,)), ((), ())), preferred_element_...  10.9 us
    all_to_all x1, blocking collectives, _balance_modes(): all_to_all(jnp.stack([original for _ in range(psum(1, 'col'))], axis=0),...  8.44 us
    dot_general x1, matrix products, per_device(): jnp.dot(_balance_modes(inverse_next), factor_column, preferred_element_ty...  6.49 us
  transfers between devices with their start and end apart: 7, of which 5 were waited for; matrix products, arithmetic and copies ran while one was open for 5% of the time, Pallas kernels for 0%

profile of v1, /device:TPU:1, one launch (start us, length us, event | category | flops | bytes accessed | tf_op | source)
XLA Modules:
  0.0 315.3 jit_solution(12135798471707156134)
XLA Ops:
  7.2 0.0 copy-start
  7.2 0.0 copy-start.6
  7.2 0.0 all-gather.8.cloned.1.call-start
  7.2 0.7 all-gather.8.cloned.1.call-update
  7.9 0.0 all-gather.6.cloned.1.call-start
  8.0 1.5 copy.13
  9.5 1.3 collective-permute-start.1
  10.8 0.0 copy-done.6
  10.8 1.3 collective-permute-start
  12.1 22.8 %collective-permute-done.1 = bf16[256,2048]{0,1:T(8,128)(2,1)S(1)} collective-permute-done((bf16[256,2048]{0,1:T(8,128)(2,1)S(1)}, bf16[256,2048]{0,1:T(8,128)(2,1)S(1)}, u32[]{:S(2)}, u32[]{:S(2)}) %collective-permute-start.1) | collective-permute-done | bytes 1048608 | tf_op jit(solution)/shard_map/ppermute | solution.py:19
  34.9 0.2 pad_maximum_fusion
  35.1 8.4 %all_to_all.24 = bf16[2,256,2048]{1,2,0:T(8,128)(2,1)S(1)} all-to-all(bf16[2,256,2048]{1,2,0:T(8,128)(2,1)S(1)} %pad_maximum_fusion), channel_id=1, replica_groups=mesh['dom'=8,'row'=16,'col'=2] {'col'}, dimensions={0} | all-to-all | bytes 4194304 | tf_op jit(solution)/shard_map/all_to_all | solution.py:10
  43.5 65.8 %all-gather.8.cloned.1.call-done = bf16[1,4096,1536]{2,1,0:T(8,128)(2,1)} async-done(((bf16[1,256,1536]{2,1,0:T(8,128)(2,1)}), bf16[1,4096,1536]{2,1,0:T(8,128)(2,1)}) %all-gather.8.cloned.1.call-update) | async-done | bytes 12582928 | tf_op jit(solution)/shard_map/all_gather | solution.py:45
  109.3 0.0 copy-start.3
  109.3 6.5 %fusion.18 = f32[256,1536]{1,0:T(8,128)S(1)} fusion(bf16[256,4096]{0,1:T(8,128)(2,1)S(1)} %bitcast.39, bf16[1,4096,1536]{2,1,0:T(8,128)(2,1)} %all-gather.8.cloned.1.call-done), kind=kOutput, calls=%fused_computation.24 | convolution fusion | flops 3221225472 | bytes 16252928 | tf_op jit(solution)/shard_map/dot_general | solution.py:48
  115.8 0.0 copy-start.2
  115.8 0.0 collective-permute-done
  115.8 0.0 copy-done.3
  115.8 1.3 fusion.4
  117.1 0.0 all-gather.6.cloned.1.call-update
  117.1 0.0 all-reduce.2.cloned.1.call-start
  117.2 0.0 copy-done.2
  117.2 1.0 fusion.9
  118.2 0.0 all-reduce.2.cloned.1.call-update
  118.2 0.0 all-gather.10.cloned.1.call-start
  118.3 0.5 all-gather.10.cloned.1.call-update
  118.8 14.1 %all-gather.6.cloned.1.call-done = bf16[256,3072]{1,0:T(8,128)(2,1)} async-done(((bf16[256,1536]{1,0:T(8,128)(2,1)}), bf16[256,3072]{1,0:T(8,128)(2,1)}) %all-gather.6.cloned.1.call-update) | async-done | bytes 1572880 | tf_op jit(solution)/shard_map/all_gather | solution.py:58
  132.9 2.6 copy.14
  135.5 0.0 copy-start.1
  135.5 6.4 %all-to-all-start.1 = ((bf16[256,16,192]{0,2,1:T(8,128)(2,1)}), bf16[256,16,192]{0,2,1:T(8,128)(2,1)S(1)}, u32[]{:S(2)}, u32[]{:S(2)}) async-start(bf16[256,16,192]{0,2,1:T(8,128)(2,1)} %bitcast.41), calls=%async_computation.1 | async-start | bytes 3145728 | tf_op jit(solution)/shard_map/all_to_all | solution.py:64
  141.9 0.0 copy-done
  141.9 0.2 fusion.20
  142.1 95.9 %all-reduce.2.cloned.1.call-done = f32[64,1536]{1,0:T(8,128)} async-done(((f32[64,1536]{1,0:T(8,128)}), f32[64,1536]{1,0:T(8,128)}) %all-reduce.2.cloned.1.call-update) | async-done | bytes 393232 | tf_op jit(solution)/shard_map/psum | solution.py:53
  238.0 1.7 negate_bitcast_fusion.1
  239.7 3.8 %all_gather.15 = bf16[64,3072]{1,0:T(8,128)(2,1)} all-gather(bf16[64,1536]{1,0:T(8,128)(2,1)S(1)} %get-tuple-element.5), channel_id=1, replica_groups=mesh['dom'=8,'row'=16,'col'=2] {'col'}, dimensions={1}, use_global_device_ids=true | all-gather | bytes 589824 | tf_op jit(solution)/shard_map/all_gather | solution.py:59
  243.5 0.0 copy-done.1
  243.5 0.0 copy-start.5
  243.5 0.9 negate_bitcast_fusion
  244.4 0.0 all-to-all-done.1
  244.4 0.2 copy.16
  244.6 53.0 %all-gather.10.cloned.1.call-done = bf16[1,4096,512]{2,1,0:T(8,128)(2,1)} async-done(((bf16[1,256,512]{2,1,0:T(8,128)(2,1)}), bf16[1,4096,512]{2,1,0:T(8,128)(2,1)}) %all-gather.10.cloned.1.call-update) | async-done | bytes 4194320 | tf_op jit(solution)/shard_map/all_gather | solution.py:65
  297.6 0.0 copy-done.5
  297.6 0.0 copy-start.4
  297.6 8.4 %fusion.5 = f32[192,2048]{1,0:T(8,128)S(1)} fusion(bf16[4096,192]{0,1:T(8,128)(2,1)S(1)} %bitcast.43, bf16[4096,512]{1,0:T(8,128)(2,1)} %bitcast.47, bf16[4096,1536]{1,0:T(8,128)(2,1)} %bitcast.38, bf16[192,512]{1,0:T(8,128)(2,1)S(1)} %bitcast.49, bf16[192,1536]{1,0:T(8,128)(2,1)} %bitcast.48), kind=kOutput, calls=%fused_computation.7 | convolution fusion | flops 3256745984 | bytes 20709376 | tf_op jit(solution)/shard_map/dot_general | solution.py:23
  305.9 0.0 copy-done.4
  306.0 1.3 fusion.8
  307.2 0.9 slice_bitcast_fusion
  308.1 0.7 slice_bitcast_fusion.1
Async XLA Ops:
  7.2 134.7 %copy-start = (bf16[64,64]{1,0:T(8,128)(2,1)S(1)}, bf16[64,64]{1,0:T(8,128)(2,1)}, u32[]{:S(2)}) copy-start(bf16[64,64]{1,0:T(8,128)(2,1)} %param.15) | copy-start | bytes 24580
  7.2 3.6 %copy-start.6 = (bf16[1,64,256]{2,1,0:T(8,128)(2,1)S(1)}, bf16[1,64,256]{2,1,0:T(8,128)(2,1)}, u32[]{:S(2)}) copy-start(bf16[1,64,256]{2,1,0:T(8,128)(2,1)} %param.10) | copy-start | bytes 98308
  7.2 102.1 %all-gather.8.cloned.1.call-start = ((), (), s32[]{:S(2)}) async-start(), calls=%async_computation.4 | async-start | bytes 13369344 | tf_op jit(solution)/shard_map/all_gather | solution.py:45
  7.9 125.0 %all-gather.6.cloned.1.call-start = ((), (), s32[]{:S(2)}) async-start(), calls=%async_computation.3 | async-start | bytes 2359296 | tf_op jit(solution)/shard_map/all_gather | solution.py:58
  9.5 25.4 %collective-permute-start.1 = (bf16[256,2048]{0,1:T(8,128)(2,1)S(1)}, bf16[256,2048]{0,1:T(8,128)(2,1)S(1)}, u32[]{:S(2)}, u32[]{:S(2)}) collective-permute-start(bf16[256,2048]{0,1:T(8,128)(2,1)S(1)} %bitcast.45), channel_id=1, source_target_pairs={{32,0},{64,32},{96,64},{128,96},{160,128},{192,160},{224,192},{33,... | collective-permute-start | bytes 3145736 | tf_op jit(solution)/shard_map/ppermute | solution.py:19
  10.8 105.1 %collective-permute-start = (bf16[64,256]{1,0:T(8,128)(2,1)S(1)}, bf16[64,256]{1,0:T(8,128)(2,1)S(1)}, u32[]{:S(2)}, u32[]{:S(2)}) collective-permute-start(bf16[64,256]{1,0:T(8,128)(2,1)S(1)} %bitcast.50), channel_id=1, source_target_pairs={{32,0},{64,32},{96,64},{128,96},{160,128},{192,160},{224,192},{33,... | collective-permute-start | bytes 98312 | tf_op jit(solution)/shard_map/ppermute | solution.py:19
  109.3 6.5 %copy-start.3 = (bf16[1,64,1536]{2,1,0:T(8,128)(2,1)S(1)}, bf16[1,64,1536]{2,1,0:T(8,128)(2,1)}, u32[]{:S(2)}) copy-start(bf16[1,64,1536]{2,1,0:T(8,128)(2,1)} %param.13) | copy-start | bytes 589828
  115.8 1.4 copy-start.2
  117.1 120.8 %all-reduce.2.cloned.1.call-start = ((), (), s32[]{:S(2)}) async-start(), calls=%async_computation.2 | async-start | bytes 786432 | tf_op jit(solution)/shard_map/psum | solution.py:53
  118.2 179.3 %all-gather.10.cloned.1.call-start = ((), (), s32[]{:S(2)}) async-start(), calls=%async_computation.5 | async-start | bytes 4456448 | tf_op jit(solution)/shard_map/all_gather | solution.py:65
  135.5 108.0 %copy-start.1 = (bf16[256,1536]{1,0:T(8,128)(2,1)S(1)}, bf16[256,1536]{1,0:T(8,128)(2,1)}, u32[]{:S(2)}) copy-start(bf16[256,1536]{1,0:T(8,128)(2,1)} %fusion.4) | copy-start | bytes 2359300
  135.5 108.9 %all-to-all-start.1 = ((bf16[256,16,192]{0,2,1:T(8,128)(2,1)}), bf16[256,16,192]{0,2,1:T(8,128)(2,1)S(1)}, u32[]{:S(2)}, u32[]{:S(2)}) async-start(bf16[256,16,192]{0,2,1:T(8,128)(2,1)} %bitcast.41), calls=%async_computation.1 | async-start | bytes 3145728 | tf_op jit(solution)/shard_map/all_to_all | solution.py:64
  243.5 54.1 %copy-start.5 = (bf16[1,192,512]{2,1,0:T(8,128)(2,1)S(1)}, bf16[1,192,512]{2,1,0:T(8,128)(2,1)}, u32[]{:S(2)}) copy-start(bf16[1,192,512]{2,1,0:T(8,128)(2,1)} %param.17) | copy-start | bytes 589828
  297.6 8.4 %copy-start.4 = (bf16[1,64,512]{2,1,0:T(8,128)(2,1)S(1)}, bf16[1,64,512]{2,1,0:T(8,128)(2,1)}, u32[]{:S(2)}) copy-start(bf16[1,64,512]{2,1,0:T(8,128)(2,1)} %param.14) | copy-start | bytes 196612
Sparse Core Ops, SparseCore 0:
  10.5 98.8 all-gather.7
  117.3 15.5 all-gather.5
  136.7 101.2 all-reduce.1
  240.3 57.2 all-gather.9
